TPU v7x, 32 devices: a whole 2x2x4 slice. The times are simulated.
32 devices in a mesh: slab: 8 (over z, y), strip: 4 (over x, core).
Axes of the slice: x: 2, y: 2, z: 4, core: 2. Of those that a mesh axis runs over, the one named last changes fastest.
Arguments:
- colors: bfloat16 [8, 4, 16, 32, 128], P('slab', 'strip'), may hold values from -6 to 6
- transmit: bfloat16 [8, 4, 16, 128], P('slab', 'strip'), may hold values from 0.099609375 to 1
- pair_counts: int32 [4, 8, 8], P('strip'), may hold values from 0 to 2, as said below
- slot_block: int32 [4, 8, 16], P('strip'), may hold values from 0 to 1023, as said below
- assign: int32 [4, 1024], P('strip'), may hold values from 0 to 1023, as said below
- depth_rank: int32 [8], replicated, may hold values from 0 to 7, each once
- w_in: bfloat16 [256, 32], replicated, may hold values from -1 to 1
- trans_weight: bfloat16 [256], replicated, may hold values from -6 to 6
- w_mid: bfloat16 [2, 256, 256], replicated, may hold values from -0.375 to 0.375
- w_out: bfloat16 [4, 256], replicated, may hold values from -0.375 to 0.375
Outputs:
- display: bfloat16 [8, 4, 128, 4, 128], P('slab', None, 'strip')
Inputs may be any that keep to these rules, and one draw needn't show every extreme that they name: pair_counts[t, s, c] counts the span blocks renderer s of strip t sends to compositor c; in every strip one compositor gets 2 from every renderer. `slot_block`: the live slots of renderer s come first, grouped by compositor in increasing order, pair_counts[t, s, c] of them for compositor c, naming distinct blocks b with assign[t, b] // 128 = c; other slots are ignored. Each strip's row is a permutation: block b goes to compositor assign[t, b] // 128 at local position assign[t, b] % 128. `depth_rank`: a permutation.
All inputs are finite; a program needn't handle non-finite values.
Results may differ from a plain program's by a relative error of at most 0.0068.
Values may be sent and summed in bfloat16 or wider, within the bound.
No kernel may reach another device: no remote copies, remote signals or barrier semaphores. Data moves between devices by JAX's collectives and lax.ppermute only.
A program may use at most 128 MiB of HBM per device.

v0:
```python
import jax
import jax.numpy as jnp
from jax import lax
from jax.sharding import PartitionSpec as P

MOST = 2
LB = 128


EXACT_PRECISION = lax.Precision.HIGHEST


def shade_blocks(blend_color, trans_field, w_in, trans_weight, w_mid, w_out):
    summed = jnp.einsum("hf,lfp->lhp", w_in, blend_color, preferred_element_type=jnp.float32)
    summed = summed + trans_weight.astype(jnp.float32)[None, :, None] * trans_field[:, None, :]
    hidden = jax.nn.silu(summed).astype(jnp.bfloat16)
    for layer_index in range(w_mid.shape[0]):
        hidden = jax.nn.silu(
            jnp.einsum(
                "hg,lgp->lhp", w_mid[layer_index], hidden, preferred_element_type=jnp.float32
            )
        ).astype(jnp.bfloat16)
    return jnp.einsum("oh,lhp->lop", w_out, hidden, preferred_element_type=jnp.float32).astype(
        jnp.bfloat16
    )


def per_device(
    colors, transmit, pair_counts, slot_block, assign, depth_rank, w_in, trans_weight, w_mid, w_out
):
    myself = lax.axis_index("slab")
    counts = pair_counts[0]
    blocks_all = slot_block[0]
    assign_row = assign[0]
    offsets = jnp.cumsum(counts, axis=1) - counts
    slot_rank = jnp.arange(MOST, dtype=jnp.int32)
    my_counts = lax.dynamic_index_in_dim(counts, myself, 0, keepdims=False)
    my_offsets = lax.dynamic_index_in_dim(offsets, myself, 0, keepdims=False)
    send_slots = jnp.where(
        slot_rank[None, :] < my_counts[:, None], my_offsets[:, None] + slot_rank[None, :], 0
    )
    send_color = colors[0, 0][send_slots]
    send_trans = transmit[0, 0][send_slots][:, :, None, :]
    incoming = lax.dynamic_index_in_dim(counts, myself, 1, keepdims=False)
    in_offsets = lax.dynamic_index_in_dim(offsets, myself, 1, keepdims=False)
    live_slot = slot_rank[None, :] < incoming[:, None]
    recv_slots = jnp.where(live_slot, in_offsets[:, None] + slot_rank[None, :], 0)
    recv_blocks = jnp.take_along_axis(blocks_all, recv_slots, axis=1)
    local_pos = assign_row[recv_blocks] - myself * LB
    live_flat = live_slot.reshape(-1)
    local_flat = jnp.where(live_flat, local_pos.reshape(-1), -1)
    depth_flat = jnp.repeat(depth_rank, MOST)
    ahead_table = (
        (local_flat[:, None] == local_flat[None, :])
        & (depth_flat[None, :] < depth_flat[:, None])
        & live_flat[None, :]
    )
    ahead_table = ahead_table.astype(jnp.float32)
    owner_table = (jnp.arange(LB, dtype=jnp.int32)[:, None] == local_flat[None, :]).astype(
        jnp.float32
    )
    got_color = lax.all_to_all(send_color, "slab", split_axis=0, concat_axis=0, tiled=True)
    got_trans = lax.all_to_all(send_trans, "slab", split_axis=0, concat_axis=0, tiled=True)
    pixel_count = got_color.shape[3]
    item_count = got_color.shape[0] * got_color.shape[1]
    log_trans = jnp.log(got_trans.reshape(item_count, pixel_count).astype(jnp.float32))
    log_trans = jnp.where(live_flat[:, None], log_trans, 0.0)
    front_log = jnp.dot(ahead_table, log_trans, precision=EXACT_PRECISION)
    front_share = jnp.where(live_flat[:, None], jnp.exp(front_log), 0.0)
    weighted = front_share[:, None, :] * got_color.reshape(item_count, -1, pixel_count).astype(
        jnp.float32
    )
    blend_sum = jnp.dot(owner_table, weighted.reshape(item_count, -1), precision=EXACT_PRECISION)
    blend_color = blend_sum.reshape(LB, -1, pixel_count).astype(jnp.bfloat16)
    trans_field = jnp.exp(jnp.dot(owner_table, log_trans, precision=EXACT_PRECISION))
    shaded = shade_blocks(blend_color, trans_field, w_in, trans_weight, w_mid, w_out)
    display_tiles = lax.all_to_all(shaded[None], "strip", split_axis=1, concat_axis=0, tiled=True)
    return display_tiles[None]


def solution(mesh):
    placed = (
        P("slab", "strip", None, None, None),
        P("slab", "strip", None, None),
        P("strip", None, None),
        P("strip", None, None),
        P("strip", None),
        P(),
        P(),
        P(),
        P(),
        P(),
    )
    return jax.shard_map(
        per_device,
        mesh=mesh,
        in_specs=placed,
        out_specs=P("slab", None, "strip", None, None),
        check_vma=False,
    )
```

profile of v0, /device:TPU:0, one launch (start us, length us, event | category | flops | bytes accessed | tf_op | source)
XLA Modules:
  0.0 69.0 jit_solution(2474098612745115591)
XLA Ops:
  0.0 0.7 %fusion.55 = s32[8]{0:T(128)S(1)} fusion(s32[1,8,8]{2,1,0:T(8,128)} %param.12, s32[]{:T(128)S(6)} %select_n.103), kind=kLoop, calls=%fused_computation.74 | loop fusion | bytes 68 | tf_op jit(solution)/shard_map/lt | solution.py:40
  0.7 0.8 %reduce_window_sum.11 = s32[8,8]{1,0:T(8,128)S(1)} reduce-window(s32[8,8]{1,0:T(8,128)} %bitcast.114, s32[]{:T(128)} %constant.44.clone.1), window={size=1x8 pad=0_0x7_0}, to_apply=%region_0.0 | reduce-window | flops 448 | bytes 516 | tf_op jit(solution)/shard_map/jit(cumsum)/reduce_window_sum | solution.py:35
  1.6 0.7 bitcast_subtract_fusion
  2.3 0.1 compare_select_fusion
  2.3 0.1 reshape.354
  2.4 1.8 %gather_fusion.1 = bf16[16,128]{1,0:T(8,128)(2,1)} fusion(bf16[16,128]{1,0:T(8,128)(2,1)} %bitcast.113, s32[1024]{0:T(1024)S(1)} %pad_clamp_fusion), kind=kCustom, calls=%fused_computation.1 | custom fusion | bytes 8256 | tf_op jit(solution)/shard_map/gather | solution.py:43
  4.3 7.3 %all-to-all-start = ((bf16[8,2,1,128]{3,1,2,0:T(2,128)(2,1)}), bf16[8,2,1,128]{3,1,2,0:T(2,128)(2,1)S(1)}, u32[]{:S(2)}, u32[]{:S(2)}) async-start(bf16[8,2,1,128]{3,1,2,0:T(2,128)(2,1)} %bitcast.8), calls=%async_computation | async-start | bytes 8192 | tf_op jit(solution)/shard_map/all_to_all | solution.py:63
  11.6 0.9 %dynamic-slice_reduce_fusion.1 = s32[8]{0:T(128)S(1)} fusion(s32[1,8,8]{2,1,0:T(8,128)} %param.12, s32[]{:T(128)S(6)} %select_n.103), kind=kLoop, calls=%fused_computation.63 | loop fusion | bytes 68 | tf_op jit(solution)/shard_map/jit(dynamic_index_in_dim)/dynamic_slice | solution.py:44
  12.4 0.2 dynamic-slice_reduce_fusion
  12.6 0.1 iota_compare_fusion.4
  12.7 0.1 lt.144
  12.8 0.1 shift-left_or_fusion
  12.9 0.1 reshape.368
  12.9 1.4 %gather_fusion.3 = s32[16]{0:T(128)S(1)} fusion(s32[8,16]{1,0:T(8,128)} %bitcast.108, s32[16]{0:T(128)S(1)} %reshape.368), kind=kCustom, calls=%fused_computation.3 | custom fusion | bytes 256 | tf_op jit(solution)/shard_map/jit(take_along_axis)/gather | solution.py:48
  14.3 0.1 gather.16
  14.4 0.1 compare_select_fusion.1
  14.5 0.1 reshape.346
  14.6 1.3 %gather_fusion = s32[16]{0:T(128)S(1)} fusion(s32[1024]{0:T(1024)} %bitcast.109, s32[1024]{0:T(1024)S(1)} %pad_clamp_fusion.1), kind=kCustom, calls=%fused_computation | custom fusion | bytes 192 | tf_op jit(solution)/shard_map/gather | solution.py:49
  15.9 0.7 convert_element_type.38
  16.6 0.7 %broadcast_in_dim.56 = s32[8,2]{1,0:T(8,128)S(1)} broadcast(s32[8]{0:T(128)} %param.15), dimensions={0} | broadcast | bytes 96 | tf_op jit(solution)/shard_map/broadcast_in_dim | solution.py:52
  17.3 0.1 lt.151
  17.4 1.2 %gather_fusion.2 = bf16[16,32,128]{2,1,0:T(8,128)(2,1)} fusion(bf16[16,32,128]{2,1,0:T(8,128)(2,1)S(1)} %bitcast.107, s32[1024]{0:T(1024)S(1)} %pad_clamp_fusion), kind=kCustom, calls=%fused_computation.2 | custom fusion | bytes 262208 | tf_op jit(solution)/shard_map/gather | solution.py:42
  18.6 6.0 %all-to-all-start.1 = ((bf16[8,2,32,128]{3,2,1,0:T(8,128)(2,1)}), bf16[8,2,32,128]{3,2,1,0:T(8,128)(2,1)S(1)}, u32[]{:S(2)}, u32[]{:S(2)}) async-start(bf16[8,2,32,128]{3,2,1,0:T(8,128)(2,1)} %bitcast.11), calls=%async_computation.1 | async-start | bytes 262144 | tf_op jit(solution)/shard_map/all_to_all | solution.py:62
  24.6 0.2 fusion.20
  24.8 0.3 convolution_exponential_fusion
  25.2 6.8 %all-to-all-done.1 = bf16[8,2,32,128]{3,2,1,0:T(8,128)(2,1)S(1)} async-done(((bf16[8,2,32,128]{3,2,1,0:T(8,128)(2,1)}), bf16[8,2,32,128]{3,2,1,0:T(8,128)(2,1)S(1)}, u32[]{:S(2)}, u32[]{:S(2)}) %all-to-all-start.1) | async-done | bytes 131104 | tf_op jit(solution)/shard_map/all_to_all | solution.py:62
  32.0 1.2 %convolution_convert_fusion = bf16[128,32,128]{2,0,1:T(8,128)(2,1)S(1)} fusion(s32[16]{0:T(128)S(1)} %subtract_select_fusion, f32[2,8,32,128]{3,2,1,0:T(8,128)S(1)} %bitcast_convert_fusion, f32[2,8,32,128]{3,2,1,0:T(8,128)S(1)} %bitcast.110), kind=kOutput, calls=%fused_computation.21 | convolution fusion | flops 101255168 | bytes 1572928 | tf_op jit(solution)/shard_map/dot_general | solution.py:73
  33.2 9.4 %multiply_convert_fusion = bf16[128,256,128]{1,2,0:T(8,128)(2,1)} fusion(f32[128,128]{1,0:T(8,128)S(1)} %convolution_exponential_fusion, f32[256]{0:T(256)S(1)} %convert_element_type.38, bf16[128,32,128]{2,0,1:T(8,128)(2,1)S(1)} %convolution_convert_fusion, bf16[256,32]{0,1:T(8,128)(2,1)} %param.16), kind=kOutput, calls=%fused_computation.15 | convolution fusion | flops 297795584 | bytes 9520128 | tf_op jit(solution)/shard_map/hf,lfp->lhp/dot_general | solution.py:14
  42.6 10.5 %fusion.8 = f32[128,128,256]{2,1,0:T(8,128)} fusion(bf16[128,256,128]{1,2,0:T(8,128)(2,1)} %multiply_convert_fusion, bf16[2,256,256]{2,1,0:T(8,128)(2,1)S(1)} %copy-done.1), kind=kOutput, calls=%fused_computation.18 | convolution fusion | flops 4315938816 | bytes 25427968 | tf_op jit(solution)/shard_map/hg,lgp->lhp/dot_general | solution.py:19
  53.1 8.1 %fusion.17 = bf16[1,128,4,128]{3,2,0,1:T(4,128)(2,1)S(1)} fusion(f32[128,128,256]{2,1,0:T(8,128)} %fusion.8, bf16[4,256]{1,0:T(4,128)(2,1)S(1)} %copy-done.2), kind=kOutput, calls=%fused_computation.23 | convolution fusion | flops 54591488 | bytes 16910336 | tf_op jit(solution)/shard_map/oh,lhp->lop/dot_general | solution.py:23
  61.2 7.2 %all_to_all.22 = bf16[1,128,4,128]{3,2,0,1:T(4,128)(2,1)S(1)} all-to-all(bf16[1,128,4,128]{3,2,0,1:T(4,128)(2,1)S(1)} %fusion.17), channel_id=1, replica_groups=mesh['slab'=8,'strip'=4] {'strip'}, dimensions={1} | all-to-all | bytes 262144 | tf_op jit(solution)/shard_map/all_to_all | solution.py:77
  68.4 0.7 copy.39
  (14 shorter events, 0.1 us)
Async XLA Ops:
  0.0 17.4 %copy-start = (bf16[1,1,16,32,128]{4,3,2,1,0:T(8,128)(2,1)S(1)}, bf16[1,1,16,32,128]{4,3,2,1,0:T(8,128)(2,1)}, u32[]{:S(2)}) copy-start(bf16[1,1,16,32,128]{4,3,2,1,0:T(8,128)(2,1)} %param.10) | copy-start | bytes 393220
  4.3 14.3 %all-to-all-start = ((bf16[8,2,1,128]{3,1,2,0:T(2,128)(2,1)}), bf16[8,2,1,128]{3,1,2,0:T(2,128)(2,1)S(1)}, u32[]{:S(2)}, u32[]{:S(2)}) async-start(bf16[8,2,1,128]{3,1,2,0:T(2,128)(2,1)} %bitcast.8), calls=%async_computation | async-start | bytes 8192 | tf_op jit(solution)/shard_map/all_to_all | solution.py:63
  18.6 13.3 %all-to-all-start.1 = ((bf16[8,2,32,128]{3,2,1,0:T(8,128)(2,1)}), bf16[8,2,32,128]{3,2,1,0:T(8,128)(2,1)S(1)}, u32[]{:S(2)}, u32[]{:S(2)}) async-start(bf16[8,2,32,128]{3,2,1,0:T(8,128)(2,1)} %bitcast.11), calls=%async_computation.1 | async-start | bytes 262144 | tf_op jit(solution)/shard_map/all_to_all | solution.py:62
  33.2 9.4 %copy-start.1 = (bf16[2,256,256]{2,1,0:T(8,128)(2,1)S(1)}, bf16[2,256,256]{2,1,0:T(8,128)(2,1)}, u32[]{:S(2)}) copy-start(bf16[2,256,256]{2,1,0:T(8,128)(2,1)} %param.18) | copy-start | bytes 786436
  42.6 10.5 %copy-start.2 = (bf16[4,256]{1,0:T(4,128)(2,1)S(1)}, bf16[4,256]{1,0:T(4,128)(2,1)}, u32[]{:S(2)}) copy-start(bf16[4,256]{1,0:T(4,128)(2,1)} %param.19) | copy-start | bytes 6148
where the time goes:
time: 69.7 us; the launch traced here: 69 us
  matrix products  29.6 us (42%)
  starting transfers between devices  13.3 us (19%)
  local copies, waits for them, and re-layouts  9.48 us (14%)
  blocking collectives  7.19 us (10%)
  waiting for transfers between devices  6.79 us (10%)
  other arithmetic  2.56 us (4%)
    dot_general x1, matrix products, shade_blocks(): jnp.einsum('hg,lgp->lhp', w_mid[layer_index], hidden, preferred_element_t...  10.5 us
    dot_general x1, matrix products, shade_blocks(): jnp.einsum('hf,lfp->lhp', w_in, blend_color, preferred_element_type=jnp.f...  9.39 us
    dot_general x1, matrix products, shade_blocks(): jnp.einsum('oh,lhp->lop', w_out, hidden, preferred_element_type=jnp.float32)  8.08 us
    all_to_all x1, starting transfers between devices, per_device(): lax.all_to_all(send_trans, 'slab', split_axis=0, concat_axis=0, tiled=True)  7.28 us
    all_to_all x1, blocking collectives, per_device(): lax.all_to_all(shaded[None], 'strip', split_axis=1, concat_axis=0, tiled=...  7.19 us
    all_to_all x1, waiting for transfers between devices, per_device(): lax.all_to_all(send_color, 'slab', split_axis=0, concat_axis=0, tiled=True)  6.79 us
    all_to_all x1, starting transfers between devices, per_device(): lax.all_to_all(send_color, 'slab', split_axis=0, concat_axis=0, tiled=True)  6 us
    gather x1, local copies, waits for them, and re-layouts, per_device(): send_trans = transmit[0, 0][send_slots][:, :, None, :]  1.85 us
  transfers between devices with their start and end apart: 2, of which 1 were waited for; matrix products, arithmetic and copies ran while one was open for 11% of the time, Pallas kernels for 0%

commit v1 on v0

--- a/solution.py
+++ b/solution.py
@@ -1,6 +1,10 @@
+import functools
+
 import jax
 import jax.numpy as jnp
 from jax import lax
+from jax.experimental import pallas as pl
+from jax.experimental.pallas import tpu as pltpu
 from jax.sharding import PartitionSpec as P
 
 MOST = 2
@@ -25,7 +29,7 @@
     )
 
 
-def per_device(
+def dense_device(
     colors, transmit, pair_counts, slot_block, assign, depth_rank, w_in, trans_weight, w_mid, w_out
 ):
     myself = lax.axis_index("slab")
@@ -78,7 +82,231 @@
     return display_tiles[None]
 
 
+SMEM = pltpu.SMEM
+VMEM = pltpu.VMEM
+
+
+def pack_kernel(
+    n_slab, counts, blocks, assign, depth, colors, transmit, table, *rest
+):
+    sends, sem = rest[:n_slab], rest[n_slab]
+    me = lax.axis_index("slab")
+    slots, feats = colors.shape[2], colors.shape[3]
+    offset = jnp.int32(0)
+    offsets = []
+    for c in range(n_slab):
+        offsets.append(offset)
+        offset = offset + counts[0, me, c]
+    copies = []
+    for k in range(n_slab):
+        peer = me ^ k
+        off = offsets[0]
+        for c in range(1, n_slab):
+            off = jnp.where(peer == c, offsets[c], off)
+        for r in range(MOST):
+            slot = jnp.minimum(off + r, slots - 1)
+            copies.append(
+                pltpu.make_async_copy(
+                    colors.at[0, 0, slot], sends[k].at[pl.ds(r * feats, feats)], sem.at[0]
+                )
+            )
+        copies.append(
+            pltpu.make_async_copy(
+                transmit.at[0, 0], sends[k].at[pl.ds(MOST * feats, slots)], sem.at[0]
+            )
+        )
+    for copy in copies:
+        copy.start()
+    pos = []
+    for k in range(n_slab):
+        peer = me ^ k
+        off = jnp.int32(0)
+        for c in range(n_slab):
+            off = off + jnp.where(c < me, counts[0, peer, c], 0)
+        count = counts[0, peer, me]
+        for r in range(MOST):
+            i = k * MOST + r
+            slot = jnp.minimum(off + r, slots - 1)
+            here = assign[0, blocks[0, peer, slot]] - me * LB
+            here = jnp.where(r < count, here, -1)
+            first = jnp.int32(i)
+            for j in reversed(range(i)):
+                first = jnp.where(pos[j] == here, j, first)
+            pos.append(here)
+            table[0, i] = here
+            table[1, i] = depth[peer]
+            table[2, i] = first
+            table[3, i] = slot
+    for copy in copies:
+        copy.wait()
+
+
+def silu_half(u):
+    return (u + u * jnp.tanh(u)).astype(jnp.bfloat16)
+
+
+def shade_kernel(n_slab, n_strip, feats, table, *refs):
+    got = refs[:n_slab]
+    w_first, w_mid, w_out = refs[n_slab : n_slab + 3]
+    pieces = refs[n_slab + 3 : n_slab + 3 + n_strip]
+    acc, tall, xs, ys = refs[n_slab + 3 + n_strip :]
+    items = n_slab * MOST
+    span = xs.shape[1] // (items + 1)
+    slots = got[0].shape[0] - MOST * feats
+    strip_me = lax.axis_index("strip")
+
+    for k in range(n_slab):
+        tall[pl.ds(k * slots, slots), :] = got[k][pl.ds(MOST * feats, slots), :].astype(jnp.float32)
+    row = lax.broadcasted_iota(jnp.int32, (items, span), 0)
+    posv = jnp.zeros((items, span), jnp.int32)
+    depthv = jnp.zeros((items, span), jnp.int32)
+    for i in range(items):
+        posv = jnp.where(row == i, table[0, i], posv)
+        depthv = jnp.where(row == i, table[1, i], depthv)
+    front = jnp.ones((items, span), jnp.float32)
+    total = jnp.ones((items, span), jnp.float32)
+    for j in range(items):
+        trans_j = tall[pl.ds((j // MOST) * slots + table[3, j], 1), :]
+        same = posv == table[0, j]
+        total = jnp.where(same, total * trans_j, total)
+        front = jnp.where(same & (depthv > table[1, j]), front * trans_j, front)
+    acc[...] = jnp.zeros_like(acc)
+    for j in range(items):
+        k, r = divmod(j, MOST)
+        color = got[k][pl.ds(r * feats, feats), :].astype(jnp.float32)
+        at = table[2, j]
+        acc[at] = acc[at] + front[j : j + 1, :] * color
+    total_hi = total.astype(jnp.bfloat16)
+    total_lo = (total - total_hi.astype(jnp.float32)).astype(jnp.bfloat16)
+    extra = xs.shape[0] - feats
+    sub = lax.broadcasted_iota(jnp.int32, (extra, span), 0)
+    for i in range(items):
+        cols = pl.ds(i * span, span)
+        xs[pl.ds(0, feats), cols] = acc[i].astype(jnp.bfloat16)
+        hi = total_hi[i : i + 1, :].astype(jnp.float32)
+        lo = total_lo[i : i + 1, :].astype(jnp.float32)
+        tail = jnp.where(sub == 0, hi, jnp.where(sub == 1, lo, 0.0))
+        xs[pl.ds(feats, extra), cols] = tail.astype(jnp.bfloat16)
+    cols = pl.ds(items * span, span)
+    xs[pl.ds(0, feats), cols] = jnp.zeros((feats, span), jnp.bfloat16)
+    xs[pl.ds(feats, extra), cols] = jnp.where(sub == 0, 1.0, 0.0).astype(jnp.bfloat16)
+
+    width = xs.shape[1]
+    step = 4 * span
+    for start in range(0, width, step):
+        size = min(step, width - start)
+        x = xs[:, pl.ds(start, size)]
+        h = silu_half(
+            lax.dot_general(
+                w_first[...], x, (((0,), (0,)), ((), ())), preferred_element_type=jnp.float32
+            )
+        )
+        for m in range(w_mid.shape[0]):
+            h = silu_half(jnp.dot(w_mid[m], h, preferred_element_type=jnp.float32))
+        y = jnp.dot(w_out[...], h, preferred_element_type=jnp.float32).astype(jnp.bfloat16)
+        for i in range(size // span):
+            ys[start // span + i] = y[:, i * span : (i + 1) * span]
+
+    tile = pieces[0].shape[0]
+    empty = jnp.broadcast_to(ys[items][None], pieces[0].shape)
+    for k in range(n_strip):
+        pieces[k][...] = empty
+    for i in range(items):
+        here = table[0, i]
+        owner = (here // tile) ^ strip_me
+        for k in range(n_strip):
+
+            @pl.when((here >= 0) & (table[2, i] == i) & (owner == k))
+            def _():
+                pieces[k][here % tile] = ys[i]
+
+
+def join_kernel(n_strip, *refs):
+    got, out, sem = refs[:n_strip], refs[n_strip], refs[n_strip + 1]
+    me = lax.axis_index("strip")
+    copies = [
+        pltpu.make_async_copy(got[k], out.at[0, me ^ k], sem.at[0]) for k in range(n_strip)
+    ]
+    for copy in copies:
+        copy.start()
+    for copy in copies:
+        copy.wait()
+
+
+def compact_device(
+    n_slab,
+    n_strip,
+    colors,
+    transmit,
+    pair_counts,
+    slot_block,
+    assign,
+    depth_rank,
+    w_in,
+    trans_weight,
+    w_mid,
+    w_out,
+):
+    slots, feats, span = colors.shape[2:]
+    items = n_slab * MOST
+    outs = w_out.shape[0]
+    buf = jax.ShapeDtypeStruct((MOST * feats + slots, span), jnp.bfloat16)
+    smem = pl.BlockSpec(memory_space=SMEM)
+    vmem = pl.BlockSpec(memory_space=VMEM)
+    anywhere = pl.BlockSpec(memory_space=pl.ANY)
+    table, *sends = pl.pallas_call(
+        functools.partial(pack_kernel, n_slab),
+        out_shape=[jax.ShapeDtypeStruct((4, items), jnp.int32)] + [buf] * n_slab,
+        in_specs=[smem] * 4 + [anywhere] * 2,
+        out_specs=[smem] + [anywhere] * n_slab,
+        scratch_shapes=[pltpu.SemaphoreType.DMA((1,))],
+        name="pack",
+    )(pair_counts, slot_block, assign, depth_rank, colors, transmit)
+    got = [sends[0]] + [
+        lax.ppermute(sends[k], "slab", [(s, s ^ k) for s in range(n_slab)])
+        for k in range(1, n_slab)
+    ]
+    hidden = w_in.shape[0]
+    extra = 16
+    w_first = jnp.concatenate(
+        [
+            w_in.T,
+            trans_weight[None],
+            trans_weight[None],
+            jnp.zeros((extra - 2, hidden), jnp.bfloat16),
+        ]
+    )
+    half = jnp.bfloat16(0.5)
+    pieces = pl.pallas_call(
+        functools.partial(shade_kernel, n_slab, n_strip, feats),
+        out_shape=[jax.ShapeDtypeStruct((LB // n_strip, outs, span), jnp.bfloat16)] * n_strip,
+        in_specs=[smem] + [vmem] * (n_slab + 3),
+        out_specs=[vmem] * n_strip,
+        scratch_shapes=[
+            pltpu.VMEM((items, feats, span), jnp.float32),
+            pltpu.VMEM((n_slab * slots, span), jnp.float32),
+            pltpu.VMEM((feats + extra, (items + 1) * span), jnp.bfloat16),
+            pltpu.VMEM((items + 1, outs, span), jnp.bfloat16),
+        ],
+        compiler_params=pltpu.CompilerParams(vmem_limit_bytes=32 * 1024 * 1024),
+        name="shade",
+    )(table, *got, w_first * half, w_mid * half, w_out)
+    tiles = [pieces[0]] + [
+        lax.ppermute(pieces[k], "strip", [(s, s ^ k) for s in range(n_strip)])
+        for k in range(1, n_strip)
+    ]
+    return pl.pallas_call(
+        functools.partial(join_kernel, n_strip),
+        out_shape=jax.ShapeDtypeStruct((1, n_strip, LB // n_strip, outs, span), jnp.bfloat16),
+        in_specs=[anywhere] * n_strip,
+        out_specs=anywhere,
+        scratch_shapes=[pltpu.SemaphoreType.DMA((1,))],
+        name="join",
+    )(*tiles)
+
+
 def solution(mesh):
+    n_slab, n_strip = mesh.shape["slab"], mesh.shape["strip"]
     placed = (
         P("slab", "strip", None, None, None),
         P("slab", "strip", None, None),
@@ -91,8 +319,10 @@
         P(),
         P(),
     )
+    powers = n_slab & (n_slab - 1) == 0 and n_strip & (n_strip - 1) == 0
+    compact = powers and 4 * MOST * n_slab <= LB
     return jax.shard_map(
-        per_device,
+        functools.partial(compact_device, n_slab, n_strip) if compact else dense_device,
         mesh=mesh,
         in_specs=placed,
         out_specs=P("slab", None, "strip", None, None),

time: 69.7 us -> 43.6 us (0.63)
  matrix products: 29.6 us -> 0 us
  Pallas kernels: 0 us -> 17.2 us
  local copies, waits for them, and re-layouts: 9.48 us -> 1.31 us
  blocking collectives: 7.19 us -> 0 us
  waiting for transfers between devices: 6.79 us -> 9.31 us
  other arithmetic: 2.56 us -> 1.07 us
  starting transfers between devices: 13.3 us -> 14.4 us
    dot_general x6 -> x0, matrix products: 29.6 us -> none  [the longest x1 10.5 us: shade_blocks(): jnp.einsum('hg,lgp->lhp', w_mid[layer_index], hidden, preferred_element_t...]
    pallas_call x0 -> x3, Pallas kernels: none -> 17.2 us  [the longest x1 7.55 us: compact_device(): pl.pallas_call(functools.partial(pack_kernel, n_slab), out_shape=[jax.Sha...]
    ppermute x0 -> x10, starting transfers between devices: none -> 14.4 us  [the longest x7 12.5 us: compact_device(): lax.ppermute(sends[k], 'slab', [(s, s ^ k) for s in range(n_slab)])]
    all_to_all x2 -> x0, starting transfers between devices: 13.3 us -> none  [the longest x1 7.28 us: per_device(): lax.all_to_all(send_trans, 'slab', split_axis=0, concat_axis=0, tiled=True)]
    ppermute x0 -> x10, waiting for transfers between devices: none -> 9.31 us  [the longest x7 6.34 us: compact_device(): lax.ppermute(sends[k], 'slab', [(s, s ^ k) for s in range(n_slab)])]
    all_to_all x1 -> x0, blocking collectives: 7.19 us -> none  [per_device(): lax.all_to_all(shaded[None], 'strip', split_axis=1, concat_axis=0, tiled=...]
    all_to_all x2 -> x0, waiting for transfers between devices: 6.79 us -> none  [the longest x1 6.79 us: per_device(): lax.all_to_all(send_color, 'slab', split_axis=0, concat_axis=0, tiled=True)]
    gather x6 -> x0, local copies, waits for them, and re-layouts: 5.95 us -> none  [the longest x1 1.85 us: per_device(): send_trans = transmit[0, 0][send_slots][:, :, None, :]]
  transfers between devices with their start and end apart: 2 -> 10, of which waited for: 1 -> 4; matrix products, arithmetic and copies ran while one was open for 11% -> 3% of each run, Pallas kernels for 0% -> 0%
where the time goes in v1:
time: 43.6 us; the launch traced here: 43.4 us
  Pallas kernels  17.2 us (39%)
  starting transfers between devices  14.4 us (33%)
  waiting for transfers between devices  9.31 us (21%)
  local copies, waits for them, and re-layouts  1.31 us (3%)
  other arithmetic  1.07 us (2%)
    ppermute x7, starting transfers between devices, compact_device(): lax.ppermute(sends[k], 'slab', [(s, s ^ k) for s in range(n_slab)])  12.5 us
    pallas_call x1, Pallas kernels, compact_device(): pl.pallas_call(functools.partial(pack_kernel, n_slab), out_shape=[jax.Sha...  7.55 us
    ppermute x7, waiting for transfers between devices, compact_device(): lax.ppermute(sends[k], 'slab', [(s, s ^ k) for s in range(n_slab)])  6.34 us
    pallas_call x1, Pallas kernels, compact_device(): pl.pallas_call(functools.partial(join_kernel, n_strip), out_shape=jax.Sha...  5.08 us
    pallas_call x1, Pallas kernels, compact_device(): pl.pallas_call(functools.partial(shade_kernel, n_slab, n_strip, feats), o...  4.6 us
    ppermute x3, waiting for transfers between devices, compact_device(): lax.ppermute(pieces[k], 'strip', [(s, s ^ k) for s in range(n_strip)])  2.97 us
    ppermute x3, starting transfers between devices, compact_device(): lax.ppermute(pieces[k], 'strip', [(s, s ^ k) for s in range(n_strip)])  1.86 us
    unnamed x22, local copies, waits for them, and re-layouts  1.23 us
  transfers between devices with their start and end apart: 10, of which 4 were waited for; matrix products, arithmetic and copies ran while one was open for 3% of the time, Pallas kernels for 0%

profile of v1, /device:TPU:0, one launch (start us, length us, event | category | flops | bytes accessed | tf_op | source)
XLA Modules:
  0.0 43.4 jit_solution(9138296744159837799)
XLA Ops:
  0.0 7.6 %pack.1 = (s32[4,16]{1,0:T(4,128)}, bf16[80,128]{1,0:T(8,128)(2,1)}, bf16[80,128]{1,0:T(8,128)(2,1)}, bf16[80,128]{1,0:T(8,128)(2,1)}, bf16[80,128]{1,0:T(8,128)...) custom-call(s32[1,8,8]{2,1,0:T(8,128)} %counts.1, ...), custom_call_target="tpu_custom_call" | custom-call | tf_op jit(solution)/shard_map/pack/pallas_call | solution.py:257
  7.6 3.0 %collective-permute-start = (bf16[80,128]{1,0:T(8,128)(2,1)}, bf16[80,128]{1,0:T(8,128)(2,1)S(1)}, u32[]{:S(2)}, u32[]{:S(2)}) collective-permute-start(bf16[80,128]{1,0:T(8,128)(2,1)} %get-tuple-element.20), channel_id=1, source_target_pairs={{0,4},{4,0},{8,12},{12,8},{16,20},{20,16},{24,28},{28,24},{1,5},{5... | collective-permute-start | bytes 61448 | tf_op jit(solution)/shard_map/ppermute | solution.py:266
  10.6 1.6 %collective-permute-start.1 = (bf16[80,128]{1,0:T(8,128)(2,1)}, bf16[80,128]{1,0:T(8,128)(2,1)S(1)}, u32[]{:S(2)}, u32[]{:S(2)}) collective-permute-start(bf16[80,128]{1,0:T(8,128)(2,1)} %get-tuple-element.21), channel_id=1, source_target_pairs={{0,8},{4,12},{8,0},{12,4},{16,24},{20,28},{24,16},{28,20},{1,9},{5... | collective-permute-start | bytes 61448 | tf_op jit(solution)/shard_map/ppermute | solution.py:266
  12.2 0.0 collective-permute-start.2
  12.2 3.0 %collective-permute-start.3 = (bf16[80,128]{1,0:T(8,128)(2,1)}, bf16[80,128]{1,0:T(8,128)(2,1)S(1)}, u32[]{:S(2)}, u32[]{:S(2)}) collective-permute-start(bf16[80,128]{1,0:T(8,128)(2,1)} %get-tuple-element.23), channel_id=1, source_target_pairs={{0,16},{4,20},{8,24},{12,28},{16,0},{20,4},{24,8},{28,12},{1,17},{... | collective-permute-start | bytes 61448 | tf_op jit(solution)/shard_map/ppermute | solution.py:266
  15.2 1.3 %collective-permute-start.4 = (bf16[80,128]{1,0:T(8,128)(2,1)}, bf16[80,128]{1,0:T(8,128)(2,1)S(1)}, u32[]{:S(2)}, u32[]{:S(2)}) collective-permute-start(bf16[80,128]{1,0:T(8,128)(2,1)} %get-tuple-element.24), channel_id=1, source_target_pairs={{0,20},{4,16},{8,28},{12,24},{16,4},{20,0},{24,12},{28,8},{1,21},{... | collective-permute-start | bytes 61448 | tf_op jit(solution)/shard_map/ppermute | solution.py:266
  16.5 1.0 %broadcast_multiply_fusion.refs_9_ = bf16[2,256,256]{2,1,0:T(8,128)(2,1)S(1)} fusion(bf16[2,256,256]{2,1,0:T(8,128)(2,1)} %param.18), kind=kLoop, calls=%fused_computation | loop fusion | flops 131072 | bytes 524288 | tf_op jit(solution)/shard_map/mul | solution.py:293
  17.4 0.0 copy-done.10
  17.5 0.1 pad.3.clone
  17.6 0.0 collective-permute-done.refs_1_
  17.6 3.6 %collective-permute-start.5 = (bf16[80,128]{1,0:T(8,128)(2,1)S(1)}, bf16[80,128]{1,0:T(8,128)(2,1)S(1)}, u32[]{:S(2)}, u32[]{:S(2)}) collective-permute-start(bf16[80,128]{1,0:T(8,128)(2,1)S(1)} %copy-done.9), channel_id=1, source_target_pairs={{0,24},{4,28},{8,16},{12,20},{16,8},{20,12},{24,0},{28,4},{1,25},{... | collective-permute-start | bytes 61448 | tf_op jit(solution)/shard_map/ppermute | solution.py:266
  21.2 0.0 collective-permute-done.1.refs_2_
  21.2 0.0 copy-done.8
  21.2 0.0 collective-permute-start.6
  21.2 0.0 copy-done.7
  21.2 0.1 maximum_multiply_fusion.refs_8_
  21.3 0.0 collective-permute-done.2.refs_3_
  21.3 0.0 collective-permute-done.3.refs_4_
  21.3 0.0 collective-permute-done.4.refs_5_
  21.3 1.8 %collective-permute-done.5.refs_6_ = bf16[80,128]{1,0:T(8,128)(2,1)S(1)} collective-permute-done((bf16[80,128]{1,0:T(8,128)(2,1)S(1)}, bf16[80,128]{1,0:T(8,128)(2,1)S(1)}, u32[]{:S(2)}, u32[]{:S(2)}) %collective-permute-start.5) | collective-permute-done | bytes 20512 | tf_op jit(solution)/shard_map/ppermute | solution.py:266
  23.2 4.5 %collective-permute-done.6.refs_7_ = bf16[80,128]{1,0:T(8,128)(2,1)S(1)} collective-permute-done((bf16[80,128]{1,0:T(8,128)(2,1)S(1)}, bf16[80,128]{1,0:T(8,128)(2,1)S(1)}, u32[]{:S(2)}, u32[]{:S(2)}) %collective-permute-start.6) | collective-permute-done | bytes 20512 | tf_op jit(solution)/shard_map/ppermute | solution.py:266
  27.7 4.6 %shade.1 = (bf16[32,4,128]{2,1,0:T(4,128)(2,1)S(1)}, bf16[32,4,128]{2,1,0:T(4,128)(2,1)S(1)}, bf16[32,4,128]{2,1,0:T(4,128)(2,1)S(1)}, bf16[32,4,128]{2,1,0:T(4,128)(2,1)S(1)}) custom-call(s32[4,16]{1,0:T(4,128)S(1)} %copy-done.3, bf16[80,128]{1,0:T(8,128)(2,1)S(1)} %copy-done.1, bf16[80,128]{1,0:T(8,128)(2,1)S(1)} %collective-permute-done.refs_1_, ...), custom_call_target="tpu_custom_call" | custom-call | tf_op jit(solution)/shard_map/shade/pallas_call | solution.py:280
  32.3 0.6 %copy-done = bf16[32,4,128]{2,1,0:T(4,128)(2,1)} copy-done((bf16[32,4,128]{2,1,0:T(4,128)(2,1)}, bf16[32,4,128]{2,1,0:T(4,128)(2,1)S(1)}, u32[]{:S(2)}) %copy-start) | copy-done | bytes 32792
  32.9 0.0 collective-permute-start.7
  32.9 1.5 %collective-permute-start.8 = (bf16[32,4,128]{2,1,0:T(4,128)(2,1)S(1)}, bf16[32,4,128]{2,1,0:T(4,128)(2,1)S(1)}, u32[]{:S(2)}, u32[]{:S(2)}) collective-permute-start(bf16[32,4,128]{2,1,0:T(4,128)(2,1)S(1)} %get-tuple-element.29), channel_id=1, source_target_pairs={{0,2},{1,3},{2,0},{3,1},{4,6},{5,7},{6,4},{7,5},{8,10},{9,11},{10,... | collective-permute-start | bytes 98312 | tf_op jit(solution)/shard_map/ppermute | solution.py:295
  34.4 0.4 collective-permute-start.9
  34.8 0.0 collective-permute-done.7.refs_1_
  34.8 2.1 %collective-permute-done.8.refs_2_ = bf16[32,4,128]{2,1,0:T(4,128)(2,1)S(1)} collective-permute-done((bf16[32,4,128]{2,1,0:T(4,128)(2,1)S(1)}, bf16[32,4,128]{2,1,0:T(4,128)(2,1)S(1)}, u32[]{:S(2)}, u32[]{:S(2)}) %collective-permute-start.8) | collective-permute-done | bytes 32800 | tf_op jit(solution)/shard_map/ppermute | solution.py:295
  36.8 0.9 %collective-permute-done.9.refs_3_ = bf16[32,4,128]{2,1,0:T(4,128)(2,1)S(1)} collective-permute-done((bf16[32,4,128]{2,1,0:T(4,128)(2,1)S(1)}, bf16[32,4,128]{2,1,0:T(4,128)(2,1)S(1)}, u32[]{:S(2)}, u32[]{:S(2)}) %collective-permute-start.9) | collective-permute-done | bytes 32800 | tf_op jit(solution)/shard_map/ppermute | solution.py:295
  37.7 0.0 copy-done.4
  37.7 0.6 %copy-done.6 = bf16[32,4,128]{2,1,0:T(4,128)(2,1)} copy-done((bf16[32,4,128]{2,1,0:T(4,128)(2,1)}, bf16[32,4,128]{2,1,0:T(4,128)(2,1)S(1)}, u32[]{:S(2)}) %copy-start.6) | copy-done | bytes 32792
  38.3 5.1 %join.1 = bf16[1,4,32,4,128]{4,3,2,1,0:T(4,128)(2,1)} custom-call(bf16[32,4,128]{2,1,0:T(4,128)(2,1)} %copy-done, bf16[32,4,128]{2,1,0:T(4,128)(2,1)} %copy-done.4, bf16[32,4,128]{2,1,0:T(4,128)(2,1)} %copy-done.5, bf16[32,4,128]{2,1,0:T(4,128)(2,1)} %copy-done.6), custom_call_target="tpu_custom_call" | custom-call | tf_op jit(solution)/shard_map/join/pallas_call | solution.py:298
  (18 shorter events, 0.0 us)
Async XLA Ops:
  7.6 10.0 %collective-permute-start = (bf16[80,128]{1,0:T(8,128)(2,1)}, bf16[80,128]{1,0:T(8,128)(2,1)S(1)}, u32[]{:S(2)}, u32[]{:S(2)}) collective-permute-start(bf16[80,128]{1,0:T(8,128)(2,1)} %get-tuple-element.20), channel_id=1, source_target_pairs={{0,4},{4,0},{8,12},{12,8},{16,20},{20,16},{24,28},{28,24},{1,5},{5... | collective-permute-start | bytes 61448 | tf_op jit(solution)/shard_map/ppermute | solution.py:266
  10.6 10.6 %collective-permute-start.1 = (bf16[80,128]{1,0:T(8,128)(2,1)}, bf16[80,128]{1,0:T(8,128)(2,1)S(1)}, u32[]{:S(2)}, u32[]{:S(2)}) collective-permute-start(bf16[80,128]{1,0:T(8,128)(2,1)} %get-tuple-element.21), channel_id=1, source_target_pairs={{0,8},{4,12},{8,0},{12,4},{16,24},{20,28},{24,16},{28,20},{1,9},{5... | collective-permute-start | bytes 61448 | tf_op jit(solution)/shard_map/ppermute | solution.py:266
  12.2 9.1 %collective-permute-start.2 = (bf16[80,128]{1,0:T(8,128)(2,1)}, bf16[80,128]{1,0:T(8,128)(2,1)S(1)}, u32[]{:S(2)}, u32[]{:S(2)}) collective-permute-start(bf16[80,128]{1,0:T(8,128)(2,1)} %get-tuple-element.22), channel_id=1, source_target_pairs={{0,12},{4,8},{8,4},{12,0},{16,28},{20,24},{24,20},{28,16},{1,13},{... | collective-permute-start | bytes 61448 | tf_op jit(solution)/shard_map/ppermute | solution.py:266
  12.2 9.2 %collective-permute-start.3 = (bf16[80,128]{1,0:T(8,128)(2,1)}, bf16[80,128]{1,0:T(8,128)(2,1)S(1)}, u32[]{:S(2)}, u32[]{:S(2)}) collective-permute-start(bf16[80,128]{1,0:T(8,128)(2,1)} %get-tuple-element.23), channel_id=1, source_target_pairs={{0,16},{4,20},{8,24},{12,28},{16,0},{20,4},{24,8},{28,12},{1,17},{... | collective-permute-start | bytes 61448 | tf_op jit(solution)/shard_map/ppermute | solution.py:266
  15.2 2.3 %copy-start.10 = (bf16[256]{0:T(256)(128)(2,1)S(1)}, bf16[256]{0:T(256)(128)(2,1)}, u32[]{:S(2)}) copy-start(bf16[256]{0:T(256)(128)(2,1)} %param.17) | copy-start | bytes 1540
  15.2 2.4 %copy-start.9 = (bf16[80,128]{1,0:T(8,128)(2,1)S(1)}, bf16[80,128]{1,0:T(8,128)(2,1)}, u32[]{:S(2)}) copy-start(bf16[80,128]{1,0:T(8,128)(2,1)} %get-tuple-element.25) | copy-start | bytes 61444
  15.2 6.0 %copy-start.8 = (bf16[80,128]{1,0:T(8,128)(2,1)S(1)}, bf16[80,128]{1,0:T(8,128)(2,1)}, u32[]{:S(2)}) copy-start(bf16[80,128]{1,0:T(8,128)(2,1)} %get-tuple-element.26) | copy-start | bytes 61444
  15.2 6.2 %collective-permute-start.4 = (bf16[80,128]{1,0:T(8,128)(2,1)}, bf16[80,128]{1,0:T(8,128)(2,1)S(1)}, u32[]{:S(2)}, u32[]{:S(2)}) collective-permute-start(bf16[80,128]{1,0:T(8,128)(2,1)} %get-tuple-element.24), channel_id=1, source_target_pairs={{0,20},{4,16},{8,28},{12,24},{16,4},{20,0},{24,12},{28,8},{1,21},{... | collective-permute-start | bytes 61448 | tf_op jit(solution)/shard_map/ppermute | solution.py:266
  16.5 4.8 %copy-start.7 = (bf16[256,32]{0,1:T(8,128)(2,1)S(1)}, bf16[256,32]{0,1:T(8,128)(2,1)}, u32[]{:S(2)}) copy-start(bf16[256,32]{0,1:T(8,128)(2,1)} %param.16) | copy-start | bytes 49156
  17.6 5.6 %collective-permute-start.5 = (bf16[80,128]{1,0:T(8,128)(2,1)S(1)}, bf16[80,128]{1,0:T(8,128)(2,1)S(1)}, u32[]{:S(2)}, u32[]{:S(2)}) collective-permute-start(bf16[80,128]{1,0:T(8,128)(2,1)S(1)} %copy-done.9), channel_id=1, source_target_pairs={{0,24},{4,28},{8,16},{12,20},{16,8},{20,12},{24,0},{28,4},{1,25},{... | collective-permute-start | bytes 61448 | tf_op jit(solution)/shard_map/ppermute | solution.py:266
  21.2 6.5 %collective-permute-start.6 = (bf16[80,128]{1,0:T(8,128)(2,1)S(1)}, bf16[80,128]{1,0:T(8,128)(2,1)S(1)}, u32[]{:S(2)}, u32[]{:S(2)}) collective-permute-start(bf16[80,128]{1,0:T(8,128)(2,1)S(1)} %copy-done.8), channel_id=1, source_target_pairs={{0,28},{4,24},{8,20},{12,16},{16,12},{20,8},{24,4},{28,0},{1,29},{... | collective-permute-start | bytes 61448 | tf_op jit(solution)/shard_map/ppermute | solution.py:266
  21.2 6.4 %copy-start.1 = (bf16[80,128]{1,0:T(8,128)(2,1)S(1)}, bf16[80,128]{1,0:T(8,128)(2,1)}, u32[]{:S(2)}) copy-start(bf16[80,128]{1,0:T(8,128)(2,1)} %get-tuple-element.19.refs_0_) | copy-start | bytes 61444
  21.2 6.4 %copy-start.3 = (s32[4,16]{1,0:T(4,128)S(1)}, s32[4,16]{1,0:T(4,128)}, u32[]{:S(2)}) copy-start(s32[4,16]{1,0:T(4,128)} %get-tuple-element.18.table) | copy-start | bytes 772
  21.3 6.4 %copy-start.2 = (bf16[4,256]{1,0:T(4,128)(2,1)S(1)}, bf16[4,256]{1,0:T(4,128)(2,1)}, u32[]{:S(2)}) copy-start(bf16[4,256]{1,0:T(4,128)(2,1)} %refs_10_.1) | copy-start | bytes 6148
  32.3 0.6 %copy-start = (bf16[32,4,128]{2,1,0:T(4,128)(2,1)}, bf16[32,4,128]{2,1,0:T(4,128)(2,1)S(1)}, u32[]{:S(2)}) copy-start(bf16[32,4,128]{2,1,0:T(4,128)(2,1)S(1)} %get-tuple-element.27.refs_0_) | copy-start | bytes 98308
  32.9 1.9 %collective-permute-start.7 = (bf16[32,4,128]{2,1,0:T(4,128)(2,1)S(1)}, bf16[32,4,128]{2,1,0:T(4,128)(2,1)S(1)}, u32[]{:S(2)}, u32[]{:S(2)}) collective-permute-start(bf16[32,4,128]{2,1,0:T(4,128)(2,1)S(1)} %get-tuple-element.28), channel_id=1, source_target_pairs={{0,1},{1,0},{2,3},{3,2},{4,5},{5,4},{6,7},{7,6},{8,9},{9,8},{10,11... | collective-permute-start | bytes 98312 | tf_op jit(solution)/shard_map/ppermute | solution.py:295
  32.9 3.9 %collective-permute-start.8 = (bf16[32,4,128]{2,1,0:T(4,128)(2,1)S(1)}, bf16[32,4,128]{2,1,0:T(4,128)(2,1)S(1)}, u32[]{:S(2)}, u32[]{:S(2)}) collective-permute-start(bf16[32,4,128]{2,1,0:T(4,128)(2,1)S(1)} %get-tuple-element.29), channel_id=1, source_target_pairs={{0,2},{1,3},{2,0},{3,1},{4,6},{5,7},{6,4},{7,5},{8,10},{9,11},{10,... | collective-permute-start | bytes 98312 | tf_op jit(solution)/shard_map/ppermute | solution.py:295
  34.4 3.3 %collective-permute-start.9 = (bf16[32,4,128]{2,1,0:T(4,128)(2,1)S(1)}, bf16[32,4,128]{2,1,0:T(4,128)(2,1)S(1)}, u32[]{:S(2)}, u32[]{:S(2)}) collective-permute-start(bf16[32,4,128]{2,1,0:T(4,128)(2,1)S(1)} %get-tuple-element.30), channel_id=1, source_target_pairs={{0,3},{1,2},{2,1},{3,0},{4,7},{5,6},{6,5},{7,4},{8,11},{9,10},{10,... | collective-permute-start | bytes 98312 | tf_op jit(solution)/shard_map/ppermute | solution.py:295
  34.8 3.0 %copy-start.4 = (bf16[32,4,128]{2,1,0:T(4,128)(2,1)}, bf16[32,4,128]{2,1,0:T(4,128)(2,1)S(1)}, u32[]{:S(2)}) copy-start(bf16[32,4,128]{2,1,0:T(4,128)(2,1)S(1)} %collective-permute-done.7.refs_1_) | copy-start | bytes 98308
  36.8 0.9 %copy-start.5 = (bf16[32,4,128]{2,1,0:T(4,128)(2,1)}, bf16[32,4,128]{2,1,0:T(4,128)(2,1)S(1)}, u32[]{:S(2)}) copy-start(bf16[32,4,128]{2,1,0:T(4,128)(2,1)S(1)} %collective-permute-done.8.refs_2_) | copy-start | bytes 98308
  37.7 0.6 %copy-start.6 = (bf16[32,4,128]{2,1,0:T(4,128)(2,1)}, bf16[32,4,128]{2,1,0:T(4,128)(2,1)S(1)}, u32[]{:S(2)}) copy-start(bf16[32,4,128]{2,1,0:T(4,128)(2,1)S(1)} %collective-permute-done.9.refs_3_) | copy-start | bytes 98308
